TPU v7x, 512 devices: a whole 4x8x8 slice. The times are simulated.
512 devices in a mesh: island: 8 (over y_lo, core), fsdp: 64 (over x, y_hi, z).
Axes of the slice: x: 4, y: 8 (y_hi: 2, y_lo: 4; y = y_hi * 4 + y_lo), z: 8, core: 2. Of those that a mesh axis runs over, the one named last changes fastest.
Arguments:
- features: bfloat16 [2, 8, 16384, 4096], P(None, 'island', 'fsdp'), may hold values from -6 to 6
- targets: bfloat16 [2, 8, 16384, 128], P(None, 'island', 'fsdp'), may hold values from -6 to 6
- labels: int32 [2, 8, 16384], P(None, 'island', 'fsdp'), may hold values from -100 to 128255
- fragment: int32 [1], replicated, may hold values from 0 to 4095
- local_weight: float32 [8, 4096, 128], P('island', 'fsdp'), may hold values from -0.09375 to 0.09375
- inner_velocity: float32 [8, 4096, 128], P('island', 'fsdp'), may hold values from -0.09375 to 0.09375
- global_weight: float32 [4096, 128], P('fsdp'), may hold values from -0.09375 to 0.09375
- outer_velocity: float32 [4096, 128], P('fsdp'), may hold values from -0.09375 to 0.09375
Outputs:
- local_out: float32 [8, 4096, 128], P('island', 'fsdp')
- velocity_out: float32 [8, 4096, 128], P('island', 'fsdp')
- global_out: float32 [4096, 128], P('fsdp')
- outer_out: float32 [4096, 128], P('fsdp')
- predictions: bfloat16 [8, 16384, 128], P('island', 'fsdp')
All inputs are finite; a program needn't handle non-finite values.
Results may differ from a plain program's by a relative error of at most 0.015.
Values may be sent and summed in bfloat16 or wider, within the bound.
A program may use at most 64 MiB of HBM per device.

v0:
```python
import jax
import jax.numpy as jnp
from jax import lax
from jax.sharding import PartitionSpec as P

FRAG = 16
FBLK = 4


INNER_RATE = 0.3
INNER_MOMENTUM = 0.9
OUTER_RATE = 0.7
OUTER_MOMENTUM = 0.9
MERGE_WEIGHT = 0.5


def as_blocks(array):
    return array.reshape(array.shape[0] // (FBLK * FRAG), FRAG, FBLK, array.shape[-1])


def select_rows(array, chosen):
    return lax.dynamic_slice_in_dim(as_blocks(array), chosen, 1, 1)


def place_rows(array, rows, chosen):
    return lax.dynamic_update_slice_in_dim(as_blocks(array), rows, chosen, 1).reshape(array.shape)


def forward_fold(features, piece):
    return jnp.dot(features, piece, preferred_element_type=jnp.float32)


def gradient_term(features, errors):
    return lax.dot_general(
        features, errors, (((0,), (0,)), ((), ())), preferred_element_type=jnp.float32
    )


def masked_errors(predicted, targets, retained):
    return (retained[:, None] * (predicted - targets.astype(jnp.float32))).astype(jnp.bfloat16)


def local(
    features, targets, labels, fragment, local_weight, inner_velocity, global_weight, outer_velocity
):
    chosen = fragment[0] % FRAG
    weight = local_weight[0]
    velocity = inner_velocity[0]
    retained = (labels[:, 0] >= 0).astype(jnp.float32)
    islands = lax.axis_size("island")
    start_rows = select_rows(global_weight, chosen)
    delta = start_rows - select_rows(weight, chosen)
    first_total = lax.psum(jnp.sum(retained[0]), "fsdp")
    first_features = features[0, 0]
    predicted = forward_fold(
        first_features, lax.all_gather(weight.astype(jnp.bfloat16), "fsdp", axis=0, tiled=True)
    )
    errors = masked_errors(predicted, targets[0, 0], retained[0])
    gradient = (
        lax.psum_scatter(
            gradient_term(first_features, errors), "fsdp", scatter_dimension=0, tiled=True
        )
        / first_total
    )
    velocity = INNER_MOMENTUM * velocity + gradient
    weight = weight - INNER_RATE * velocity
    summed = lax.psum(delta, "island")
    outer_mean = summed / islands
    outer_rows = OUTER_MOMENTUM * select_rows(outer_velocity, chosen) + outer_mean
    global_rows = start_rows - OUTER_RATE * (OUTER_MOMENTUM * outer_rows + outer_mean)
    merged = MERGE_WEIGHT * global_rows + (1.0 - MERGE_WEIGHT) * select_rows(weight, chosen)
    weight = place_rows(weight, merged, chosen)
    second_total = lax.psum(jnp.sum(retained[1]), "fsdp")
    second_features = features[1, 0]
    predicted = forward_fold(
        second_features, lax.all_gather(weight.astype(jnp.bfloat16), "fsdp", axis=0, tiled=True)
    )
    errors = masked_errors(predicted, targets[1, 0], retained[1])
    gradient = (
        lax.psum_scatter(
            gradient_term(second_features, errors), "fsdp", scatter_dimension=0, tiled=True
        )
        / second_total
    )
    velocity = INNER_MOMENTUM * velocity + gradient
    weight = weight - INNER_RATE * velocity
    return (
        weight[None],
        velocity[None],
        place_rows(global_weight, global_rows, chosen),
        place_rows(outer_velocity, outer_rows, chosen),
        predicted.astype(jnp.bfloat16)[None],
    )


def solution(mesh):
    return jax.shard_map(
        local,
        mesh=mesh,
        in_specs=(
            P(None, "island", "fsdp", None),
            P(None, "island", "fsdp", None),
            P(None, "island", "fsdp"),
            P(),
            P("island", "fsdp", None),
            P("island", "fsdp", None),
            P("fsdp", None),
            P("fsdp", None),
        ),
        out_specs=(
            P("island", "fsdp", None),
            P("island", "fsdp", None),
            P("fsdp", None),
            P("fsdp", None),
            P("island", "fsdp", None),
        ),
        check_vma=False,
    )
```

profile of v0, /device:TPU:8, one launch (start us, length us, event | category | flops | bytes accessed | tf_op | source)
XLA Modules:
  0.0 1168.3 jit_solution(2824513274693226405)
XLA Ops:
  7.2 0.0 all-gather.3.cloned.1.call-start
  7.2 0.8 copy.50
  8.0 1.4 bitcast_convert_fusion
  9.3 0.0 all-gather.3.cloned.1.call-update
  9.4 0.0 reduce-scatter.7.cloned.1.call-start
  9.4 0.7 compare_convert_fusion
  10.1 0.6 slice_reduce_fusion
  10.7 133.5 %all-gather.3.cloned.1.call-done = bf16[4096,128]{1,0:T(8,128)(2,1)} async-done(((bf16[64,128]{1,0:T(8,128)(2,1)}), bf16[4096,128]{1,0:T(8,128)(2,1)}) %all-gather.3.cloned.1.call-update) | async-done | bytes 1048592 | tf_op jit(solution)/shard_map/all_gather | solution.py:56
  144.2 3.7 convolution_bitcast_fusion.1
  147.9 1.9 copy.39
  149.8 0.0 reduce-scatter.7.cloned.1.call-update
  149.8 0.0 all-gather.5.cloned.1.call-start
  149.9 220.9 %all-reduce = (f32[]{:T(128)}, f32[]{:T(128)}) all-reduce(f32[]{:T(128)} %get-tuple-element.21, f32[]{:T(128)} %get-tuple-element.20), channel_id=1, replica_groups=mesh['island'=8,'fsdp'=64] {'fsdp'}, use_global_device_ids=true, to_apply=%region_2.3 | all-reduce | flops 2 | bytes 16 | tf_op jit(solution)/shard_map/psum | solution.py:53
  371.5 0.0 copy-done
  371.5 10.9 psum.22
  382.3 208.1 %reduce-scatter.7.cloned.1.call-done = f32[64,128]{1,0:T(8,128)} async-done(((f32[4096,128]{1,0:T(8,128)}), f32[64,128]{1,0:T(8,128)}) %reduce-scatter.7.cloned.1.call-update) | async-done | bytes 32784 | tf_op jit(solution)/shard_map/reduce_scatter | solution.py:60
  590.5 1.4 bitcast_subtract_fusion
  591.9 0.0 copy-start.1
  592.0 0.0 copy-start.2
  592.0 0.6 convert_element_type.36
  592.6 0.0 all-gather.5.cloned.1.call-update
  592.6 0.0 reduce-scatter.9.cloned.1.call-start
  592.7 0.0 slice-done
  592.7 0.1 copy.43
  592.8 119.8 %all-gather.5.cloned.1.call-done = bf16[4096,128]{1,0:T(8,128)(2,1)} async-done(((bf16[64,128]{1,0:T(8,128)(2,1)}), bf16[4096,128]{1,0:T(8,128)(2,1)}) %all-gather.5.cloned.1.call-update) | async-done | bytes 1048592 | tf_op jit(solution)/shard_map/all_gather | solution.py:76
  712.6 2.7 fusion.10
  715.3 2.0 convolution_bitcast_fusion
  717.4 1.9 copy.41
  719.3 0.0 reduce-scatter.9.cloned.1.call-update
  719.3 0.7 copy.38
  720.0 439.8 %reduce-scatter.9.cloned.1.call-done = f32[64,128]{1,0:T(8,128)} async-done(((f32[4096,128]{1,0:T(8,128)}), f32[64,128]{1,0:T(8,128)}) %reduce-scatter.9.cloned.1.call-update) | async-done | bytes 32784 | tf_op jit(solution)/shard_map/reduce_scatter | solution.py:80
  1159.8 2.0 fusion.33
  (11 shorter events, 0.1 us)
Async XLA Ops:
  7.2 137.0 %all-gather.3.cloned.1.call-start = ((), (), s32[]{:S(2)}) async-start(), calls=%async_computation.2 | async-start | bytes 1064960 | tf_op jit(solution)/shard_map/all_gather | solution.py:56
  9.4 581.1 %reduce-scatter.7.cloned.1.call-start = ((), (), s32[]{:S(2)}) async-start(), calls=%async_computation.4 | async-start | bytes 2129920 | tf_op jit(solution)/shard_map/reduce_scatter | solution.py:60
  149.8 221.7 %copy-start = (f32[1,64,128]{2,1,0:T(8,128)S(1)}, f32[1,64,128]{2,1,0:T(8,128)}, u32[]{:S(2)}) copy-start(f32[1,64,128]{2,1,0:T(8,128)} %param.12) | copy-start | bytes 98308
  149.8 440.7 %copy-start.4 = (f32[1,64,128]{2,1,0:T(8,128)S(1)}, f32[1,64,128]{2,1,0:T(8,128)}, u32[]{:S(2)}) copy-start(f32[1,64,128]{2,1,0:T(8,128)} %param.13) | copy-start | bytes 98308
  149.8 442.1 %copy-start.3 = (f32[64,128]{1,0:T(8,128)S(1)}, f32[64,128]{1,0:T(8,128)}, u32[]{:S(2)}) copy-start(f32[64,128]{1,0:T(8,128)} %param.15) | copy-start | bytes 98308
  149.8 442.9 %slice-start = ((bf16[2,1,256,128]{3,2,1,0:T(8,128)(2,1)}), bf16[1,1,256,128]{3,2,1,0:T(8,128)(2,1)S(1)}, s32[]{:S(2)}) async-start(bf16[2,1,256,128]{3,2,1,0:T(8,128)(2,1)} %param.9), calls=%async_computation.6 | async-start | bytes 131072 | tf_op jit(solution)/shard_map/slice | solution.py:78
  149.8 562.8 %all-gather.5.cloned.1.call-start = ((), (), s32[]{:S(2)}) async-start(), calls=%async_computation.3 | async-start | bytes 1064960 | tf_op jit(solution)/shard_map/all_gather | solution.py:76
  591.9 125.4 %copy-start.1 = (f32[1,16,4,128]{3,2,1,0:T(4,128)}, f32[1,16,4,128]{3,2,1,0:T(4,128)S(1)}, u32[]{:S(2)}) copy-start(f32[1,16,4,128]{3,2,1,0:T(4,128)S(1)} %get-tuple-element.26) | copy-start | bytes 98308
  592.0 125.4 %copy-start.2 = (f32[1,16,4,128]{3,2,1,0:T(4,128)}, f32[1,16,4,128]{3,2,1,0:T(4,128)S(1)}, u32[]{:S(2)}) copy-start(f32[1,16,4,128]{3,2,1,0:T(4,128)S(1)} %get-tuple-element.30) | copy-start | bytes 98308
  592.6 567.2 %reduce-scatter.9.cloned.1.call-start = ((), (), s32[]{:S(2)}) async-start(), calls=%async_computation.5 | async-start | bytes 2129920 | tf_op jit(solution)/shard_map/reduce_scatter | solution.py:80
Sparse Core Ops, SparseCore 0:
  12.9 131.1 all-gather.2
  149.9 440.5 reduce-scatter.6
  596.2 116.3 all-gather.4
  719.4 440.3 reduce-scatter.8
where the time goes:
time: 1170 us
  waiting for transfers between devices  901 us (77%)
  blocking collectives  232 us (20%)
  between operations  14.5 us (1%)
    reduce_scatter x1, waiting for transfers between devices, local(): lax.psum_scatter(gradient_term(second_features, errors), 'fsdp', scatter_...  440 us
    all_gather x2, waiting for transfers between devices, local(): lax.all_gather(weight.astype(jnp.bfloat16), 'fsdp', axis=0, tiled=True)  253 us
    psum x1, blocking collectives, local(): first_total = lax.psum(jnp.sum(retained[0]), 'fsdp')  221 us
    reduce_scatter x1, waiting for transfers between devices, local(): lax.psum_scatter(gradient_term(first_features, errors), 'fsdp', scatter_d...  208 us
  transfers between devices with their start and end apart: 4, of which 4 were waited for; matrix products, arithmetic and copies ran while one was open for 0% of the time, Pallas kernels for 0%

commit v1 on v0

v1 whole, which is shorter than its diff:
```python
import functools

import jax
import jax.numpy as jnp
from jax import lax
from jax.experimental import pallas as pl
from jax.experimental.pallas import tpu as pltpu
from jax.sharding import PartitionSpec as P

FRAG = 16
FBLK = 4

INNER_RATE = 0.3
INNER_MOMENTUM = 0.9
OUTER_RATE = 0.7
OUTER_MOMENTUM = 0.9
MERGE_WEIGHT = 0.5

NX, NY, NZ = 4, 2, 8
MESH = pl.DeviceIdType.MESH


def near_first(i):
    h = i // 2 + 1
    return h + (i % 2) * (NZ - 2 * h)


def far_first(i):
    return near_first(NZ - 2 - i)


def kernel(
    islands,
    frag_ref, feat_ref, tgt_ref, lab_ref, w_ref, v_ref, gw_ref, ov_ref,
    w_out, v_out, g_out, o_out, p_out,
    xbuf, wg, grad, gb, rx, sz, rz, sy, ry, cbuf, cz, cx, cy, dbuf, dz, keep,
    feat_sem, zs, zr, xs, xr, ys, yr, bxs, bxr, bzs, bzr, bys, byr,
    czs, czr, cxs, cxr, cys, cyr, ds_, dr,
):
    f32, bf16 = jnp.float32, jnp.bfloat16
    f = lax.axis_index("fsdp")
    isl = lax.axis_index("island")
    x, y, z = f // (NY * NZ), (f // NZ) % NY, f % NZ
    other = 1 - y

    def dev(dx=0, dy=0, dz_=0):
        return {"fsdp": (((x + dx) % NX) * NY + (y + dy) % NY) * NZ + (z + dz_) % NZ}

    def peer(i):
        return {"island": (isl + i) % islands}

    def remote(src, dst, ss, rs, to):
        return pltpu.make_async_remote_copy(src, dst, ss, rs, device_id=to, device_id_type=MESH)

    def loop(n, body, start=0):
        def step(i, c):
            body(i)
            return c
        lax.fori_loop(start, n, step, 0)

    feats = [pltpu.make_async_copy(feat_ref.at[s, 0], xbuf.at[s], feat_sem.at[s]) for s in range(2)]
    for c in feats:
        c.start()

    barrier = pltpu.get_barrier_semaphore()

    def greet(to):
        pl.semaphore_signal(barrier, inc=1, device_id=to, device_id_type=MESH)

    loop(NZ, lambda d: greet(dev(dz_=d)), 1)
    loop(NX, lambda d: greet(dev(dx=d)), 1)
    greet(dev(dy=1))
    loop(islands, lambda i: greet(peer(i)), 1)

    wg[0, x, y, z] = w_ref[0].astype(bf16)
    retained = [(lab_ref[s] >= 0).astype(f32) for s in range(2)]
    halves = [r[:, :128] + r[:, 128:] for r in retained]
    row8 = lax.broadcasted_iota(jnp.int32, (8, 128), 0)
    cbuf[0] = jnp.where(row8 == 0, halves[0], jnp.where(row8 == 1, halves[1], 0.0))
    chosen = frag_ref[0] & (FRAG - 1)
    rows = lax.broadcasted_iota(jnp.int32, (64, 128), 0)
    mine = (rows // FBLK) == chosen
    diff = jnp.where(mine, gw_ref[...] - w_ref[0], 0.0)
    dbuf[...] = jnp.sum(diff.reshape(8, 8, 128), axis=0)

    pl.semaphore_wait(barrier, (NZ - 1) + (NX - 1) + 1 + (islands - 1))

    def which(k):
        return (y + k) % NY

    def ag_y(s):
        blk = wg.at[s, x, y, z]
        return remote(blk, blk, ys.at[s], yr.at[s], dev(dy=1))

    def ag_z(s, k, d):
        blk = wg.at[s, x, which(k), z]
        return remote(blk, blk, zs.at[s, k, d], zr.at[s, k, d], dev(dz_=d))

    def ag_x(s, k, d, dx):
        blk = wg.at[s, x, which(k), (z + NZ - d) % NZ]
        return remote(blk, blk, xs.at[s, k, d, dx], xr.at[s, k, d, dx], dev(dx=dx))

    def ag_open(s, k):
        loop(NZ - 1, lambda i: ag_z(s, k, far_first(i)).start())
        for dx in (2, 1, 3):
            ag_x(s, k, 0, dx).start()

    def ag_pass(s, k, lo, hi):
        def body(i):
            d = near_first(i)
            ag_z(s, k, d).wait_recv()
            for dx in (2, 1, 3):
                ag_x(s, k, d, dx).start()
        loop(hi, body, lo)

    def ag_wait(s, k):
        def body(d):
            for dx in (1, 3, 2):
                ag_x(s, k, d, dx).wait_recv()
        loop(NZ, body)

    def ag_begin(s):
        ag_y(s).start()
        ag_open(s, 0)

    def ag_middle(s):
        ag_pass(s, 0, 0, 4)
        ag_y(s).wait_recv()
        ag_open(s, 1)
        ag_pass(s, 0, 4, NZ - 1)
        ag_pass(s, 1, 0, NZ - 1)

    def count_z(d):
        return remote(cbuf.at[0], cz.at[d], czs.at[d], czr.at[d], dev(dz_=d))

    def count_x(d):
        return remote(cbuf.at[1], cx.at[d], cxs.at[d], cxr.at[d], dev(dx=d))

    def count_y():
        return remote(cbuf.at[2], cy, cys, cyr, dev(dy=1))

    def outer(i):
        return remote(dbuf, dz.at[i], ds_.at[i], dr.at[i], peer(i))

    def rs_x(s, k, d, dx):
        zz = (z + d) % NZ
        return remote(
            gb.at[s, (x + dx) % NX, which(k), zz], rx.at[s, k, d, dx],
            bxs.at[s, k, d, dx], bxr.at[s, k, d, dx], dev(dx=dx),
        )

    def rs_z(s, k, d):
        return remote(sz.at[s, k, d], rz.at[s, k, d], bzs.at[s, k, d], bzr.at[s, k, d], dev(dz_=d))

    def rs_y(s):
        return remote(sy.at[s], ry.at[s], bys.at[s], byr.at[s], dev(dy=1))

    def columns(xx, yy):
        return pl.ds(pl.multiple_of((xx * NY + yy) * (NZ * 64), NZ * 64), NZ * 64)

    def forward(s, k, acc):
        def body(xx, acc):
            yy = which(k)
            piece = wg[s, xx, yy].reshape(NZ * 64, 128)
            return acc + jnp.dot(xbuf[s, :, columns(xx, yy)], piece, preferred_element_type=f32)
        return lax.fori_loop(0, NX, body, acc)

    def reduce(s, errors):
        for k in (1, 0):
            def block(i):
                dx = (NX + 2 - i) % NX
                xx, yy = (x + dx) % NX, which(k)
                part = lax.dot_general(
                    xbuf[s, :, columns(xx, yy)], errors, (((0,), (0,)), ((), ())),
                    preferred_element_type=f32,
                ).reshape(NZ, 64, 128)
                return dx, xx, yy, part

            for i in (0, 1, 3):
                dx, xx, yy, part = block(i)
                gb[s, xx, yy] = part.astype(bf16)
                loop(NZ - 1, lambda j: rs_x(s, k, far_first(j), dx).start())
                rs_x(s, k, 0, dx).start()
            dx, xx, yy, part = block(2)
            grad[k] = part
        for k in (1, 0):
            def total(d):
                for dx in (1, 3, 2):
                    rs_x(s, k, d, dx).wait_recv()
                t = grad[k, (z + d) % NZ]
                for dx in (1, 2, 3):
                    t = t + rx[s, k, d, dx].astype(f32)
                return t

            def body(j):
                d = far_first(j)
                sz[s, k, d] = total(d).astype(bf16)
                rs_z(s, k, d).start()
            loop(NZ - 1, body)
            keep[k] = total(0)

        def plane(k):
            def body(d, t):
                rs_z(s, k, d).wait_recv()
                return t + rz[s, k, d].astype(f32)
            return lax.fori_loop(1, NZ, body, keep[k])
        sy[s] = plane(1).astype(bf16)
        rs_y(s).start()
        t = plane(0)
        rs_y(s).wait_recv()
        return t + ry[s].astype(f32)

    def mask_of(s):
        return jnp.broadcast_to(retained[s], (128, 256)).T

    def errors_of(s, predicted):
        return (mask_of(s) * (predicted - tgt_ref[s, 0].astype(f32))).astype(bf16)

    ag_begin(0)
    loop(islands, lambda i: outer(i).start(), 1)
    loop(NZ, lambda d: count_z(d).start(), 1)
    ag_middle(0)

    def count_sum(d, t):
        count_z(d).wait_recv()
        return t + cz[d]
    cbuf[1] = lax.fori_loop(1, NZ, count_sum, cbuf[0])
    loop(NX, lambda d: count_x(d).start(), 1)

    feats[0].wait()
    ag_wait(0, 0)
    acc = forward(0, 0, jnp.zeros((256, 128), f32))

    def count_sum_x(d, t):
        count_x(d).wait_recv()
        return t + cx[d]
    cbuf[2] = lax.fori_loop(1, NX, count_sum_x, cbuf[1])
    count_y().start()

    ag_wait(0, 1)
    acc = forward(0, 1, acc)
    gradient = reduce(0, errors_of(0, acc))

    count_y().wait_recv()
    counts = cbuf[2] + cy[...]
    first_total = jnp.sum(jnp.where(row8 == 0, counts, 0.0))
    second_total = jnp.sum(jnp.where(row8 == 1, counts, 0.0))

    def outer_sum(i, t):
        outer(i).wait_recv()
        return t + dz[i]
    summed = lax.fori_loop(1, islands, outer_sum, dbuf[...])
    outer_mean = jnp.broadcast_to((summed / islands)[None], (8, 8, 128)).reshape(64, 128)
    outer_rows = OUTER_MOMENTUM * ov_ref[...] + outer_mean
    global_rows = gw_ref[...] - OUTER_RATE * (OUTER_MOMENTUM * outer_rows + outer_mean)
    g_out[...] = jnp.where(mine, global_rows, gw_ref[...])
    o_out[...] = jnp.where(mine, outer_rows, ov_ref[...])

    velocity = INNER_MOMENTUM * v_ref[0] + gradient / first_total
    weight = w_ref[0] - INNER_RATE * velocity
    weight = jnp.where(mine, MERGE_WEIGHT * global_rows + (1.0 - MERGE_WEIGHT) * weight, weight)
    wg[1, x, y, z] = weight.astype(bf16)

    ag_begin(1)
    v_out[0] = velocity
    w_out[0] = weight
    ag_middle(1)
    feats[1].wait()
    ag_wait(1, 0)
    acc = forward(1, 0, jnp.zeros((256, 128), f32))
    ag_wait(1, 1)
    acc = forward(1, 1, acc)
    p_out[0] = acc.astype(bf16)
    gradient = reduce(1, errors_of(1, acc))
    velocity = INNER_MOMENTUM * v_out[0] + gradient / second_total
    v_out[0] = velocity
    w_out[0] = w_out[0] - INNER_RATE * velocity

    for s in range(2):
        ag_y(s).wait_send()
        rs_y(s).wait_send()
        for k in range(2):
            def sent_z(d):
                ag_z(s, k, d).wait_send()
                rs_z(s, k, d).wait_send()
            loop(NZ, sent_z, 1)

            def sent_x(d):
                for dx in (1, 2, 3):
                    ag_x(s, k, d, dx).wait_send()
                    rs_x(s, k, d, dx).wait_send()
            loop(NZ, sent_x)
    loop(NZ, lambda d: count_z(d).wait_send(), 1)
    loop(NX, lambda d: count_x(d).wait_send(), 1)
    count_y().wait_send()
    loop(islands, lambda i: outer(i).wait_send(), 1)


def local(
    features, targets, labels, fragment, local_weight, inner_velocity, global_weight, outer_velocity
):
    islands = lax.axis_size("island")
    f32, bf16 = jnp.float32, jnp.bfloat16
    vmem = pl.BlockSpec(memory_space=pltpu.VMEM)
    dma, V = pltpu.SemaphoreType.DMA, pltpu.VMEM
    return pl.pallas_call(
        functools.partial(kernel, islands),
        out_shape=(
            jax.ShapeDtypeStruct((1, 64, 128), f32),
            jax.ShapeDtypeStruct((1, 64, 128), f32),
            jax.ShapeDtypeStruct((64, 128), f32),
            jax.ShapeDtypeStruct((64, 128), f32),
            jax.ShapeDtypeStruct((1, 256, 128), bf16),
        ),
        in_specs=[
            pl.BlockSpec(memory_space=pltpu.SMEM), pl.BlockSpec(memory_space=pl.ANY),
            vmem, vmem, vmem, vmem, vmem, vmem,
        ],
        out_specs=(vmem,) * 5,
        scratch_shapes=[
            V((2, 256, 4096), bf16),
            V((2, NX, NY, NZ, 64, 128), bf16),
            V((2, NZ, 64, 128), f32),
            V((2, NX, NY, NZ, 64, 128), bf16),
            V((2, 2, NZ, NX, 64, 128), bf16),
            V((2, 2, NZ, 64, 128), bf16),
            V((2, 2, NZ, 64, 128), bf16),
            V((2, 64, 128), bf16),
            V((2, 64, 128), bf16),
            V((3, 8, 128), f32),
            V((NZ, 8, 128), f32),
            V((NX, 8, 128), f32),
            V((8, 128), f32),
            V((8, 128), f32),
            V((islands, 8, 128), f32),
            V((2, 64, 128), f32),
            dma((2,)),
            dma((2, 2, NZ)), dma((2, 2, NZ)),
            dma((2, 2, NZ, NX)), dma((2, 2, NZ, NX)),
            dma((2,)), dma((2,)),
            dma((2, 2, NZ, NX)), dma((2, 2, NZ, NX)),
            dma((2, 2, NZ)), dma((2, 2, NZ)),
            dma((2,)), dma((2,)),
            dma((NZ,)), dma((NZ,)), dma((NX,)), dma((NX,)), dma, dma,
            dma((islands,)), dma((islands,)),
        ],
        compiler_params=pltpu.CompilerParams(
            collective_id=0, has_side_effects=True, vmem_limit_bytes=40 << 20
        ),
        cost_estimate=pl.CostEstimate(flops=1 << 30, bytes_accessed=5 << 20, transcendentals=0),
    )(fragment, features, targets, labels, local_weight, inner_velocity, global_weight, outer_velocity)


def solution(mesh):
    return jax.shard_map(
        local,
        mesh=mesh,
        in_specs=(
            P(None, "island", "fsdp", None),
            P(None, "island", "fsdp", None),
            P(None, "island", "fsdp"),
            P(),
            P("island", "fsdp", None),
            P("island", "fsdp", None),
            P("fsdp", None),
            P("fsdp", None),
        ),
        out_specs=(
            P("island", "fsdp", None),
            P("island", "fsdp", None),
            P("fsdp", None),
            P("fsdp", None),
            P("island", "fsdp", None),
        ),
        check_vma=False,
    )
```

time: 1170 us -> 102 us (0.09)
  the two profiles are of different devices: /device:TPU:8 before, /device:TPU:6 now
where the time goes in v1:
time: 102 us; the launch traced here: 101 us
  Pallas kernels  89.6 us (88%)
  local copies, waits for them, and re-layouts  9.88 us (10%)
  between operations  1.3 us (1%)
    pallas_call x1, Pallas kernels, local(): pl.pallas_call(functools.partial(kernel, islands), out_shape=(jax.ShapeDt...  89.6 us
    unnamed x19, local copies, waits for them, and re-layouts  9.88 us

profile of v1, /device:TPU:6, one launch (start us, length us, event | category | flops | bytes accessed | tf_op | source)
XLA Modules:
  0.0 100.8 jit_solution(1162723378485990240)
XLA Ops:
  1.3 0.0 copy-start
  1.3 2.2 %copy-done = bf16[2,1,256,4096]{3,2,1,0:T(8,128)(2,1)S(1)} copy-done((bf16[2,1,256,4096]{3,2,1,0:T(8,128)(2,1)S(1)}, bf16[2,1,256,4096]{3,2,1,0:T(8,128)(2,1)}, u32[]{:S(2)}) %copy-start) | copy-done | bytes 4194328
  3.5 0.0 copy-start.1
  3.5 0.9 copy-done.1
  4.4 0.0 copy-start.2
  4.4 0.8 copy-done.2
  5.1 0.0 copy-start.3
  5.1 0.8 copy-done.3
  5.9 0.0 copy-start.4
  5.9 0.8 copy-done.4
  6.6 0.0 copy-start.5
  6.7 0.8 copy-done.5
  7.4 0.0 copy-start.6
  7.4 0.7 copy-done.6
  8.1 89.6 %shard_map.119 = (f32[1,64,128]{2,1,0:T(8,128)S(1)}, f32[1,64,128]{2,1,0:T(8,128)S(1)}, f32[64,128]{1,0:T(8,128)S(1)}, f32[64,128]{1,0:T(8,128)S(1)}, bf16[1,256,128]{2,1,0:T(8,128)(2,1)S(1)}) custom-call(s32[1]{0:T(128)S(6)} %copy.18.frag_ref, bf16[2,1,256,4096]{3,2,1,0:T(8,128)(2,1)S(1)} %copy-done, bf16[2,1,256,128]{3,2,1,0:T(8,128)(2,1)S(1)} %copy-done.1, ...), custom_call_target="tpu_custom_call" | custom-call | flops 1073741824 | bytes 5242880 | tf_op jit(solution)/shard_map/pallas_call | solution.py:306
  97.7 0.6 copy.19
  98.3 0.6 copy.20
  98.9 0.6 copy.21
  99.5 0.6 copy.22
  100.2 0.6 copy.23
Async XLA Ops:
  1.3 2.2 %copy-start = (bf16[2,1,256,4096]{3,2,1,0:T(8,128)(2,1)S(1)}, bf16[2,1,256,4096]{3,2,1,0:T(8,128)(2,1)}, u32[]{:S(2)}) copy-start(bf16[2,1,256,4096]{3,2,1,0:T(8,128)(2,1)} %feat_ref.1) | copy-start | bytes 12582916
  3.5 0.9 copy-start.1
  4.4 0.8 copy-start.2
  5.1 0.8 copy-start.3
  5.9 0.8 copy-start.4
  6.6 0.8 copy-start.5
  7.4 0.7 copy-start.6

commit v2 on v0

v2 whole, which is shorter than its diff:
```python
import functools

import jax
import jax.numpy as jnp
from jax import lax
from jax.experimental import pallas as pl
from jax.experimental.pallas import tpu as pltpu
from jax.sharding import PartitionSpec as P

FRAG = 16
FBLK = 4

INNER_RATE = 0.3
INNER_MOMENTUM = 0.9
OUTER_RATE = 0.7
OUTER_MOMENTUM = 0.9
MERGE_WEIGHT = 0.5

NX, NY, NZ = 4, 2, 8
MESH = pl.DeviceIdType.MESH


OFF = (0, 1, 7, 2, 6, 3, 5, 4)
GROUPS = ((0, 3), (3, 8))
STREAMS = 2
HALF = 64


def turned(a):
    return pltpu.roll(a, HALF, 1)


def kernel(
    islands,
    frag_ref, feat_hbm, tgt_hbm, lab_hbm, w_hbm, v_hbm, gw_hbm, ov_hbm,
    w_out, v_out, g_out, o_out, p_out,
    tgt_ref, lab_ref, w_ref, v_ref, gw_ref, ov_ref,
    xbuf, wg, piece, grad, gb, rx, sz, rz, sy, ry, cbuf, cz, cx, cy, dbuf, dz, keep,
    wf, vf, gf, mask, pred,
    load_sem, feat_sem, zs, zr, xs, xr, ys, yr, bxs, bxr, bzs, bzr, bys, byr,
    small_s, small_r,
):
    f32, bf16 = jnp.float32, jnp.bfloat16
    f = lax.axis_index("fsdp")
    isl = lax.axis_index("island")
    x, y, z = f // (NY * NZ), (f // NZ) % NY, f % NZ

    def dev(dx=0, dy=0, dz_=0):
        return {"fsdp": (((x + dx) % NX) * NY + (y + dy) % NY) * NZ + (z + dz_) % NZ}

    def peer(i):
        return {"island": (isl + i) % islands}

    def remote(src, dst, ss, rs, to):
        return pltpu.make_async_remote_copy(src, dst, ss, rs, device_id=to, device_id_type=MESH)

    def loop(n, body, start=0):
        def step(i, c):
            body(i)
            return c
        lax.fori_loop(start, n, step, 0)

    pairs = (
        (w_hbm, w_ref), (lab_hbm, lab_ref), (gw_hbm, gw_ref), (v_hbm, v_ref), (ov_hbm, ov_ref), (tgt_hbm, tgt_ref),
    )
    loads = [pltpu.make_async_copy(a, b, load_sem.at[i]) for i, (a, b) in enumerate(pairs)]
    feats = [pltpu.make_async_copy(feat_hbm.at[s, 0], xbuf.at[s], feat_sem.at[s]) for s in range(2)]

    barrier = pltpu.get_barrier_semaphore()

    def greet(to):
        pl.semaphore_signal(barrier, inc=1, device_id=to, device_id_type=MESH)

    loop(NZ, lambda d: greet(dev(dz_=d)), 1)
    loop(NX, lambda d: greet(dev(dx=d)), 1)
    greet(dev(dy=1))
    loop(islands, lambda i: greet(peer(i)), 1)
    for c in loads + feats:
        c.start()
    for c in loads:
        c.wait()

    lane32 = lax.broadcasted_iota(jnp.int32, (32, 128), 1)
    lane = lax.broadcasted_iota(jnp.int32, (256, 128), 1)

    def fold(a, c):
        low, high = a[:32], a[32:]
        if c == 0:
            return jnp.where(lane32 < HALF, low, turned(high))
        return jnp.where(lane32 < HALF, turned(low), high)

    def unfold(a, b):
        return jnp.concatenate([
            jnp.where(lane32 < HALF, a, turned(b)), jnp.where(lane32 < HALF, turned(a), b),
        ], axis=0)

    for c in range(STREAMS):
        wf[c] = fold(w_ref[0], c)
        wg[0, c, x, 0, 0] = wf[c].astype(bf16)
        vf[c] = fold(v_ref[0], c)
    retained = [(lab_ref[s] >= 0).astype(f32) for s in range(2)]
    halves = [r[:, :128] + r[:, 128:] for r in retained]
    row8 = lax.broadcasted_iota(jnp.int32, (8, 128), 0)
    cbuf[0] = jnp.where(row8 == 0, halves[0], jnp.where(row8 == 1, halves[1], 0.0))
    chosen = frag_ref[0] & (FRAG - 1)
    rows = lax.broadcasted_iota(jnp.int32, (64, 128), 0)
    mine = (rows // FBLK) == chosen
    rows32 = lax.broadcasted_iota(jnp.int32, (32, 128), 0) + jnp.where(lane32 < HALF, 0, 32)
    mine_folded = (rows32 // FBLK) == chosen
    diff = jnp.where(mine, gw_ref[...] - w_ref[0], 0.0)
    dbuf[...] = jnp.sum(diff.reshape(8, 8, 128), axis=0)

    pl.semaphore_wait(barrier, (NZ - 1) + (NX - 1) + 1 + (islands - 1))

    def which(k):
        return (y + k) % NY

    def ag_y(s, c):
        return remote(wg.at[s, c, x, 0, 0], wg.at[s, c, x, 1, 0], ys.at[c], yr.at[s, c], dev(dy=1))

    def ag_z(s, c, k, i):
        g = [lo <= i < hi for lo, hi in GROUPS].index(True)
        return remote(
            wg.at[s, c, x, k, 0], wg.at[s, c, x, k, i], zs.at[c, k], zr.at[s, c, k, g], dev(dz_=NZ - OFF[i])
        )

    def ag_x(s, c, k, g, dx):
        blk = wg.at[s, c, x, k, pl.ds(GROUPS[g][0], GROUPS[g][1] - GROUPS[g][0])]
        return remote(blk, blk, xs.at[c, k], xr.at[s, c, k], dev(dx=dx))

    def all_of(ref, ss, rs):
        return remote(ref, ref, ss, rs, dev(dx=1))

    def ag_open(s, c, k):
        for i in range(NZ - 1, 0, -1):
            ag_z(s, c, k, i).start()

    def ag_pass(s, c, k, groups=range(len(GROUPS))):
        for g in groups:
            lo, hi = GROUPS[g]
            first = max(lo, 1)
            if first < hi:
                all_of(wg.at[s, c, x, k, pl.ds(first, hi - first)], zs.at[c, k], zr.at[s, c, k, g]).wait_recv()
            for dx in (2, 1, 3):
                ag_x(s, c, k, g, dx).start()

    def ag_wait(s, c, k):
        all_of(wg.at[s, c, pl.ds(0, NX - 1), k], xs.at[c, k], xr.at[s, c, k]).wait_recv()

    def ag_begin(s, c):
        ag_y(s, c).start()
        ag_open(s, c, 0)

    def ag_turn(s, c):
        ag_y(s, c).wait_recv()
        ag_open(s, c, 1)

    def count_z(d):
        return remote(cbuf.at[0], cz.at[d], small_s.at[0], small_r.at[0], dev(dz_=d))

    def count_x(d):
        return remote(cbuf.at[1], cx.at[d], small_s.at[1], small_r.at[1], dev(dx=d))

    def count_y():
        return remote(cbuf.at[2], cy, small_s.at[2], small_r.at[2], dev(dy=1))

    def outer(i):
        return remote(dbuf, dz.at[i], small_s.at[3], small_r.at[3], peer(i))

    def all_small(j):
        ref, n = ((cz, NZ), (cx, NX), None, (dz, islands))[j]
        return all_of(ref.at[pl.ds(1, n - 1)], small_s.at[j], small_r.at[j])

    def rs_x(s, c, k, g, dx):
        part = pl.ds(GROUPS[g][0], GROUPS[g][1] - GROUPS[g][0])
        return remote(
            gb.at[s, c, (x + dx) % NX, k, part], rx.at[s, c, k, dx, part],
            bxs.at[c, k], bxr.at[s, c, k, g], dev(dx=dx),
        )

    def rs_z(s, c, k, i):
        return remote(sz.at[s, c, k, i], rz.at[s, c, k, i], bzs.at[c, k], bzr.at[s, c, k], dev(dz_=OFF[i]))

    def rs_y(s, c):
        return remote(sy.at[s, c], ry.at[s, c], bys.at[c], byr.at[s, c], dev(dy=1))

    def columns(xx, yy):
        return pl.ds(pl.multiple_of((xx * NY + yy) * (NZ * 64), NZ * 64), NZ * 64)

    def forward(s, c, k, acc):
        def body(xx, acc):
            for i in range(NZ):
                at = pl.multiple_of(((z + OFF[i]) % NZ) * 64, 64)
                block = wg[s, c, xx, k, i]
                piece[xx, pl.ds(at, 32)] = block
                piece[xx, pl.ds(at + 32, 32)] = turned(block.astype(f32)).astype(bf16)
            return acc + jnp.dot(xbuf[s, :, columns(xx, which(k))], piece[xx], preferred_element_type=f32)
        return lax.fori_loop(0, NX, body, acc)

    def spread(s, c, errors):
        for k in (1, 0):
            def block(dx):
                xx = (x + dx) % NX
                part = lax.dot_general(
                    xbuf[s, :, columns(xx, which(k))], errors, (((0,), (0,)), ((), ())),
                    preferred_element_type=f32,
                ).reshape(NZ, 2, 32, 128)
                low, high = part[:, 0].reshape(NZ * 32, 128), part[:, 1].reshape(NZ * 32, 128)
                folded = (low + turned(high)).reshape(NZ, 32, 128)
                for zz in range(NZ):
                    e = (zz - z + NZ) % NZ
                    slot = jnp.where(e == 0, 0, jnp.where(e <= NZ // 2, 2 * e - 1, 2 * (NZ - e)))
                    yield xx, slot, folded[zz]

            for dx in (2, 1, 3):
                for xx, slot, part in block(dx):
                    gb[s, c, xx, k, slot] = part.astype(bf16)
                for g in reversed(range(len(GROUPS))):
                    rs_x(s, c, k, g, dx).start()
            for _, slot, part in block(0):
                grad[c, k, slot] = part

    def gather_terms(s, c, k):
        for g in reversed(range(len(GROUPS))):
            lo, hi = GROUPS[g]
            part = rx.at[s, c, k, pl.ds(1, NX - 1), pl.ds(lo, hi - lo)]
            all_of(part, bxs.at[c, k], bxr.at[s, c, k, g]).wait_recv()
            t = grad[c, k, lo:hi]
            for dx in (1, 2, 3):
                t = t + rx[s, c, k, dx, lo:hi].astype(f32)
            sz[s, c, k, lo:hi] = t.astype(bf16)
            if lo == 0:
                keep[c, k] = t[0]
            for i in range(hi - 1, max(lo, 1) - 1, -1):
                rs_z(s, c, k, i).start()

    def plane(s, c, k):
        t = keep[c, k]
        all_of(rz.at[s, c, k, pl.ds(1, NZ - 1)], bzs.at[c, k], bzr.at[s, c, k]).wait_recv()
        for i in range(1, NZ):
            t = t + rz[s, c, k, i].astype(f32)
        return t

    def far_sum(s, c):
        sy[s, c] = plane(s, c, 1).astype(bf16)
        rs_y(s, c).start()

    def own_sum(s, c):
        t = plane(s, c, 0)
        rs_y(s, c).wait_recv()
        return t + ry[s, c].astype(f32)

    def errors_of(s, c, predicted):
        target = tgt_ref[s, 0].astype(f32)
        if c:
            target = turned(target)
        return jnp.where(lane < HALF, mask[s] * (predicted - target), 0.0).astype(bf16)

    def compute(s, c):
        acc = jnp.zeros((256, 128), f32)
        for k in range(2):
            ag_wait(s, c, k)
            acc = forward(s, c, k, acc)
        if s == 1:
            pred[c] = acc
        spread(s, c, errors_of(s, c, acc))

    def sent_gather(s, c):
        ag_y(s, c).wait_send()
        for k in range(2):
            all_of(wg.at[s, c, x, k, pl.ds(1, NZ - 1)], zs.at[c, k], zr.at[s, c, k, 0]).wait_send()
            all_of(wg.at[s, c, pl.ds(0, NX - 1), k], xs.at[c, k], xr.at[s, c, k]).wait_send()

    def sent_sum(s, c):
        rs_y(s, c).wait_send()
        for k in range(2):
            all_of(sz.at[s, c, k, pl.ds(1, NZ - 1)], bzs.at[c, k], bzr.at[s, c, k]).wait_send()
            all_of(gb.at[s, c, pl.ds(0, NX - 1), k], bxs.at[c, k], bxr.at[s, c, k, 0]).wait_send()

    both = range(STREAMS)

    def middle(s):
        for c in both:
            ag_pass(s, c, 0)
        for c in both:
            ag_turn(s, c)
        for c in both:
            ag_pass(s, c, 1)

    for c in both:
        ag_begin(0, c)
    loop(islands, lambda i: outer(i).start(), 1)
    loop(NZ, lambda d: count_z(d).start(), 1)
    for s in range(2):
        mask[s] = jnp.broadcast_to(retained[s], (128, 256)).T
    middle(0)

    all_small(0).wait_recv()
    cbuf[1] = cbuf[0] + jnp.sum(cz[1:], axis=0)
    loop(NX, lambda d: count_x(d).start(), 1)

    all_small(3).wait_recv()
    summed = dbuf[...] + jnp.sum(dz[1:], axis=0)
    outer_mean = jnp.broadcast_to((summed / islands)[None], (8, 8, 128)).reshape(64, 128)
    outer_rows = OUTER_MOMENTUM * ov_ref[...] + outer_mean
    global_rows = gw_ref[...] - OUTER_RATE * (OUTER_MOMENTUM * outer_rows + outer_mean)
    g_out[...] = jnp.where(mine, global_rows, gw_ref[...])
    o_out[...] = jnp.where(mine, outer_rows, ov_ref[...])
    for c in both:
        gf[c] = fold(global_rows, c)

    feats[0].wait()
    compute(0, 0)

    all_small(1).wait_recv()
    cbuf[2] = cbuf[1] + jnp.sum(cx[1:], axis=0)
    count_y().start()

    compute(0, 1)
    for c in both:
        for k in (1, 0):
            gather_terms(0, c, k)
    for c in both:
        far_sum(0, c)

    count_y().wait_recv()
    counts = cbuf[2] + cy[...]
    first_total = jnp.sum(jnp.where(row8 == 0, counts, 0.0))
    second_total = jnp.sum(jnp.where(row8 == 1, counts, 0.0))

    for c in both:
        sent_gather(0, c)
    for c in both:
        velocity = INNER_MOMENTUM * vf[c] + own_sum(0, c) / first_total
        weight = wf[c] - INNER_RATE * velocity
        weight = jnp.where(mine_folded, MERGE_WEIGHT * gf[c] + (1.0 - MERGE_WEIGHT) * weight, weight)
        wg[1, c, x, 0, 0] = weight.astype(bf16)
        ag_begin(1, c)
        vf[c] = velocity
        wf[c] = weight

    middle(1)
    for c in both:
        sent_sum(0, c)
    feats[1].wait()
    for c in both:
        compute(1, c)
    p_out[0] = jnp.where(lane < HALF, pred[0], turned(pred[1])).astype(bf16)
    for c in both:
        for k in (1, 0):
            gather_terms(1, c, k)
    for c in both:
        sent_gather(1, c)
    for j in (0, 1, 3):
        all_small(j).wait_send()
    count_y().wait_send()
    for c in both:
        far_sum(1, c)
    for c in both:
        velocity = INNER_MOMENTUM * vf[c] + own_sum(1, c) / second_total
        vf[c] = velocity
        wf[c] = wf[c] - INNER_RATE * velocity
    w_out[0] = unfold(wf[0], wf[1])
    v_out[0] = unfold(vf[0], vf[1])
    for c in both:
        sent_sum(1, c)


def write_out(*refs):
    ins, outs, held, (arrived, left) = refs[:5], refs[5:10], refs[10:15], refs[15:]
    loads = [pltpu.make_async_copy(a, b, arrived.at[i]) for i, (a, b) in enumerate(zip(ins, held))]
    stores = [pltpu.make_async_copy(a, b, left.at[i]) for i, (a, b) in enumerate(zip(held, outs))]
    for c in loads:
        c.start()
    for a, b in zip(loads, stores):
        a.wait()
        b.start()
    for c in stores:
        c.wait()


def local(
    features, targets, labels, fragment, local_weight, inner_velocity, global_weight, outer_velocity
):
    islands = lax.axis_size("island")
    f32, bf16 = jnp.float32, jnp.bfloat16
    vmem = pl.BlockSpec(memory_space=pltpu.VMEM)
    hbm = pl.BlockSpec(memory_space=pltpu.HBM)
    dma, V, C, G = pltpu.SemaphoreType.DMA, pltpu.VMEM, STREAMS, len(GROUPS)
    results = pl.pallas_call(
        functools.partial(kernel, islands),
        out_shape=(
            jax.ShapeDtypeStruct((1, 64, 128), f32),
            jax.ShapeDtypeStruct((1, 64, 128), f32),
            jax.ShapeDtypeStruct((64, 128), f32),
            jax.ShapeDtypeStruct((64, 128), f32),
            jax.ShapeDtypeStruct((1, 256, 128), bf16),
        ),
        in_specs=[
            pl.BlockSpec(memory_space=pltpu.SMEM), hbm, hbm, hbm, hbm, hbm, hbm, hbm,
        ],
        out_specs=(vmem,) * 5,
        scratch_shapes=[
            V((2, 1, 256, 128), bf16),
            V((2, 1, 256), jnp.int32),
            V((1, 64, 128), f32), V((1, 64, 128), f32),
            V((64, 128), f32), V((64, 128), f32),
            V((2, 256, 4096), bf16),
            V((2, C, NX, NY, NZ, 32, 128), bf16),
            V((NX, NZ * 64, 128), bf16),
            V((C, 2, NZ, 32, 128), f32),
            V((2, C, NX, NY, NZ, 32, 128), bf16),
            V((2, C, 2, NX, NZ, 32, 128), bf16),
            V((2, C, 2, NZ, 32, 128), bf16),
            V((2, C, 2, NZ, 32, 128), bf16),
            V((2, C, 32, 128), bf16),
            V((2, C, 32, 128), bf16),
            V((3, 8, 128), f32),
            V((NZ, 8, 128), f32),
            V((NX, 8, 128), f32),
            V((8, 128), f32),
            V((8, 128), f32),
            V((islands, 8, 128), f32),
            V((C, 2, 32, 128), f32),
            V((C, 32, 128), f32), V((C, 32, 128), f32), V((C, 32, 128), f32),
            V((2, 256, 128), f32), V((C, 256, 128), f32),
            dma((6,)), dma((2,)),
            dma((C, 2)), dma((2, C, 2, G)),
            dma((C, 2)), dma((2, C, 2)),
            dma((C,)), dma((2, C)),
            dma((C, 2)), dma((2, C, 2, G)),
            dma((C, 2)), dma((2, C, 2)),
            dma((C,)), dma((2, C)),
            dma((4,)), dma((4,)),
        ],
        compiler_params=pltpu.CompilerParams(
            collective_id=0, has_side_effects=True, vmem_limit_bytes=63 << 20
        ),
        cost_estimate=pl.CostEstimate(flops=1 << 30, bytes_accessed=5 << 20, transcendentals=0),
    )(fragment, features, targets, labels, local_weight, inner_velocity, global_weight, outer_velocity)
    return pl.pallas_call(
        write_out,
        out_shape=[jax.ShapeDtypeStruct(r.shape, r.dtype) for r in results],
        in_specs=[hbm] * 5,
        out_specs=[hbm] * 5,
        scratch_shapes=[V(r.shape, r.dtype) for r in results] + [dma((5,)), dma((5,))],
        compiler_params=pltpu.CompilerParams(vmem_limit_bytes=63 << 20),
    )(*results)


def solution(mesh):
    return jax.shard_map(
        local,
        mesh=mesh,
        in_specs=(
            P(None, "island", "fsdp", None),
            P(None, "island", "fsdp", None),
            P(None, "island", "fsdp"),
            P(),
            P("island", "fsdp", None),
            P("island", "fsdp", None),
            P("fsdp", None),
            P("fsdp", None),
        ),
        out_specs=(
            P("island", "fsdp", None),
            P("island", "fsdp", None),
            P("fsdp", None),
            P("fsdp", None),
            P("island", "fsdp", None),
        ),
        check_vma=False,
    )
```

time: 1170 us -> 90.9 us (0.08)
  the two profiles are of different devices: /device:TPU:8 before, /device:TPU:6 now
where the time goes in v2:
time: 90.9 us; the launch traced here: 90.7 us
  Pallas kernels  89.4 us (98%)
  between operations  1.29 us (1%)
    pallas_call x1, Pallas kernels, local(): pl.pallas_call(functools.partial(kernel, islands), out_shape=(jax.ShapeDt...  87.8 us

profile of v2, /device:TPU:6, one launch (start us, length us, event | category | flops | bytes accessed | tf_op | source)
XLA Modules:
  0.0 90.7 jit_solution(2389294364889090637)
XLA Ops:
  1.3 87.8 %shard_map.119 = (f32[1,64,128]{2,1,0:T(8,128)}, f32[1,64,128]{2,1,0:T(8,128)}, f32[64,128]{1,0:T(8,128)}, f32[64,128]{1,0:T(8,128)}, bf16[1,256,128]{2,1,0:T(8,128)(2,1)}) custom-call(s32[1]{0:T(128)S(6)} %copy.13.frag_ref, bf16[2,1,256,4096]{3,2,1,0:T(8,128)(2,1)} %feat_hbm.1, bf16[2,1,256,128]{3,2,1,0:T(8,128)(2,1)} %tgt_hbm.1, s32[2,1,256]{2,1,0:T(1,128)} %lab_hbm.1, ...), custom_call_target="tpu_custom_call" | custom-call | flops 1073741824 | bytes 5242880 | tf_op jit(solution)/shard_map/pallas_call | solution.py:390
  89.1 1.6 %shard_map.120 = (f32[1,64,128]{2,1,0:T(8,128)}, f32[1,64,128]{2,1,0:T(8,128)}, f32[64,128]{1,0:T(8,128)}, f32[64,128]{1,0:T(8,128)}, bf16[1,256,128]{2,1,0:T(8,128)(2,1)}) custom-call(f32[1,64,128]{2,1,0:T(8,128)} %get-tuple-element.10.refs_0_, f32[1,64,128]{2,1,0:T(8,128)} %get-tuple-element.11.refs_1_, f32[64,128]{1,0:T(8,128)} %get-tuple-element.12.refs_2_, ...), custom_call_target="tpu_custom_call" | custom-call | tf_op jit(solution)/shard_map/pallas_call | solution.py:441

commit v3 on v2

--- a/solution.py
+++ b/solution.py
@@ -21,7 +21,8 @@
 
 
 OFF = (0, 1, 7, 2, 6, 3, 5, 4)
-GROUPS = ((0, 3), (3, 8))
+GROUPS = ((0, 1), (1, 3), (3, 5), (5, 8))
+NEAR = 2
 STREAMS = 2
 HALF = 64
 
@@ -36,7 +37,7 @@
     w_out, v_out, g_out, o_out, p_out,
     tgt_ref, lab_ref, w_ref, v_ref, gw_ref, ov_ref,
     xbuf, wg, piece, grad, gb, rx, sz, rz, sy, ry, cbuf, cz, cx, cy, dbuf, dz, keep,
-    wf, vf, gf, mask, pred,
+    wf, vf, gf, mask, pred, err,
     load_sem, feat_sem, zs, zr, xs, xr, ys, yr, bxs, bxr, bzs, bzr, bys, byr,
     small_s, small_r,
 ):
@@ -132,7 +133,7 @@
         return remote(ref, ref, ss, rs, dev(dx=1))
 
     def ag_open(s, c, k):
-        for i in range(NZ - 1, 0, -1):
+        for i in range(1, NZ):
             ag_z(s, c, k, i).start()
 
     def ag_pass(s, c, k, groups=range(len(GROUPS))):
@@ -197,28 +198,28 @@
             return acc + jnp.dot(xbuf[s, :, columns(xx, which(k))], piece[xx], preferred_element_type=f32)
         return lax.fori_loop(0, NX, body, acc)
 
-    def spread(s, c, errors):
-        for k in (1, 0):
-            def block(dx):
-                xx = (x + dx) % NX
-                part = lax.dot_general(
-                    xbuf[s, :, columns(xx, which(k))], errors, (((0,), (0,)), ((), ())),
-                    preferred_element_type=f32,
-                ).reshape(NZ, 2, 32, 128)
-                low, high = part[:, 0].reshape(NZ * 32, 128), part[:, 1].reshape(NZ * 32, 128)
-                folded = (low + turned(high)).reshape(NZ, 32, 128)
-                for zz in range(NZ):
-                    e = (zz - z + NZ) % NZ
-                    slot = jnp.where(e == 0, 0, jnp.where(e <= NZ // 2, 2 * e - 1, 2 * (NZ - e)))
-                    yield xx, slot, folded[zz]
-
-            for dx in (2, 1, 3):
-                for xx, slot, part in block(dx):
-                    gb[s, c, xx, k, slot] = part.astype(bf16)
-                for g in reversed(range(len(GROUPS))):
-                    rs_x(s, c, k, g, dx).start()
-            for _, slot, part in block(0):
-                grad[c, k, slot] = part
+    def terms(s, c, k, dx):
+        xx = (x + dx) % NX
+        part = lax.dot_general(
+            xbuf[s, :, columns(xx, which(k))], err[c], (((0,), (0,)), ((), ())), preferred_element_type=f32
+        ).reshape(NZ, 2, 32, 128)
+        low, high = part[:, 0].reshape(NZ * 32, 128), part[:, 1].reshape(NZ * 32, 128)
+        folded = (low + turned(high)).reshape(NZ, 32, 128)
+        for zz in range(NZ):
+            e = (zz - z + NZ) % NZ
+            slot = jnp.where(e == 0, 0, jnp.where(e <= NZ // 2, 2 * e - 1, 2 * (NZ - e)))
+            yield xx, slot, folded[zz]
+
+    def spread(s, c, k):
+        for dx in (2, 1, 3):
+            for xx, slot, part in terms(s, c, k, dx):
+                gb[s, c, xx, k, slot] = part.astype(bf16)
+            for g in reversed(range(len(GROUPS))):
+                rs_x(s, c, k, g, dx).start()
+
+    def own_terms(s, c, k):
+        for _, slot, part in terms(s, c, k, 0):
+            grad[c, k, slot] = part
 
     def gather_terms(s, c, k):
         for g in reversed(range(len(GROUPS))):
@@ -263,7 +264,8 @@
             acc = forward(s, c, k, acc)
         if s == 1:
             pred[c] = acc
-        spread(s, c, errors_of(s, c, acc))
+        err[c] = errors_of(s, c, acc)
+        spread(s, c, 1)
 
     def sent_gather(s, c):
         ag_y(s, c).wait_send()
@@ -281,14 +283,18 @@
 
     def middle(s):
         for c in both:
-            ag_pass(s, c, 0)
+            ag_pass(s, c, 0, range(NEAR))
         for c in both:
             ag_turn(s, c)
         for c in both:
+            ag_pass(s, c, 0, range(NEAR, len(GROUPS)))
+        for c in both:
             ag_pass(s, c, 1)
 
     for c in both:
-        ag_begin(0, c)
+        ag_y(0, c).start()
+    for c in both:
+        ag_open(0, c, 0)
     loop(islands, lambda i: outer(i).start(), 1)
     loop(NZ, lambda d: count_z(d).start(), 1)
     for s in range(2):
@@ -318,7 +324,12 @@
 
     compute(0, 1)
     for c in both:
-        for k in (1, 0):
+        spread(0, c, 0)
+    for k in (1, 0):
+        for c in both:
+            own_terms(0, c, k)
+    for k in (1, 0):
+        for c in both:
             gather_terms(0, c, k)
     for c in both:
         far_sum(0, c)
@@ -347,7 +358,12 @@
         compute(1, c)
     p_out[0] = jnp.where(lane < HALF, pred[0], turned(pred[1])).astype(bf16)
     for c in both:
-        for k in (1, 0):
+        spread(1, c, 0)
+    for k in (1, 0):
+        for c in both:
+            own_terms(1, c, k)
+    for k in (1, 0):
+        for c in both:
             gather_terms(1, c, k)
     for c in both:
         sent_gather(1, c)
@@ -424,6 +440,7 @@
             V((C, 2, 32, 128), f32),
             V((C, 32, 128), f32), V((C, 32, 128), f32), V((C, 32, 128), f32),
             V((2, 256, 128), f32), V((C, 256, 128), f32),
+            V((C, 256, 128), bf16),
             dma((6,)), dma((2,)),
             dma((C, 2)), dma((2, C, 2, G)),
             dma((C, 2)), dma((2, C, 2)),

time: 90.9 us -> 85.7 us (0.943)
  Pallas kernels: 89.4 us -> 83.6 us
    pallas_call x1, Pallas kernels: 87.8 us -> 81.9 us  [local(): pl.pallas_call(functools.partial(kernel, islands), out_shape=(jax.ShapeDt...]
where the time goes in v3:
time: 85.7 us; the launch traced here: 84.8 us
  Pallas kernels  83.6 us (98%)
  between operations  1.29 us (2%)
    pallas_call x1, Pallas kernels, local(): pl.pallas_call(functools.partial(kernel, islands), out_shape=(jax.ShapeDt...  81.9 us

profile of v3, /device:TPU:6, one launch (start us, length us, event | category | flops | bytes accessed | tf_op | source)
XLA Modules:
  0.0 84.8 jit_solution(1810248634873516174)
XLA Ops:
  1.3 81.9 %shard_map.119 = (f32[1,64,128]{2,1,0:T(8,128)}, f32[1,64,128]{2,1,0:T(8,128)}, f32[64,128]{1,0:T(8,128)}, f32[64,128]{1,0:T(8,128)}, bf16[1,256,128]{2,1,0:T(8,128)(2,1)}) custom-call(s32[1]{0:T(128)S(6)} %copy.13.frag_ref, bf16[2,1,256,4096]{3,2,1,0:T(8,128)(2,1)} %feat_hbm.1, bf16[2,1,256,128]{3,2,1,0:T(8,128)(2,1)} %tgt_hbm.1, s32[2,1,256]{2,1,0:T(1,128)} %lab_hbm.1, ...), custom_call_target="tpu_custom_call" | custom-call | flops 1073741824 | bytes 5242880 | tf_op jit(solution)/shard_map/pallas_call | solution.py:406
  83.2 1.6 %shard_map.120 = (f32[1,64,128]{2,1,0:T(8,128)}, f32[1,64,128]{2,1,0:T(8,128)}, f32[64,128]{1,0:T(8,128)}, f32[64,128]{1,0:T(8,128)}, bf16[1,256,128]{2,1,0:T(8,128)(2,1)}) custom-call(f32[1,64,128]{2,1,0:T(8,128)} %get-tuple-element.10.refs_0_, f32[1,64,128]{2,1,0:T(8,128)} %get-tuple-element.11.refs_1_, f32[64,128]{1,0:T(8,128)} %get-tuple-element.12.refs_2_, ...), custom_call_target="tpu_custom_call" | custom-call | tf_op jit(solution)/shard_map/pallas_call | solution.py:458

commit v4 on v3

--- a/solution.py
+++ b/solution.py
@@ -21,7 +21,7 @@
 
 
 OFF = (0, 1, 7, 2, 6, 3, 5, 4)
-GROUPS = ((0, 1), (1, 3), (3, 5), (5, 8))
+GROUPS = ((0, 1), (1, 3), (3, 5), (5, 7), (7, 8))
 NEAR = 2
 STREAMS = 2
 HALF = 64

time: 85.7 us -> 85.4 us (level)
  no operation moved by 1% of the time
where the time goes in v4:
time: 85.4 us; the launch traced here: 84.8 us
  Pallas kernels  83.5 us (98%)
  between operations  1.29 us (2%)
    pallas_call x1, Pallas kernels, local(): pl.pallas_call(functools.partial(kernel, islands), out_shape=(jax.ShapeDt...  81.9 us

profile of v4, /device:TPU:6, one launch (start us, length us, event | category | flops | bytes accessed | tf_op | source)
XLA Modules:
  0.0 84.8 jit_solution(11803980079672884874)
XLA Ops:
  1.3 81.9 %shard_map.119 = (f32[1,64,128]{2,1,0:T(8,128)}, f32[1,64,128]{2,1,0:T(8,128)}, f32[64,128]{1,0:T(8,128)}, f32[64,128]{1,0:T(8,128)}, bf16[1,256,128]{2,1,0:T(8,128)(2,1)}) custom-call(s32[1]{0:T(128)S(6)} %copy.13.frag_ref, bf16[2,1,256,4096]{3,2,1,0:T(8,128)(2,1)} %feat_hbm.1, bf16[2,1,256,128]{3,2,1,0:T(8,128)(2,1)} %tgt_hbm.1, s32[2,1,256]{2,1,0:T(1,128)} %lab_hbm.1, ...), custom_call_target="tpu_custom_call" | custom-call | flops 1073741824 | bytes 5242880 | tf_op jit(solution)/shard_map/pallas_call | solution.py:406
  83.2 1.6 %shard_map.120 = (f32[1,64,128]{2,1,0:T(8,128)}, f32[1,64,128]{2,1,0:T(8,128)}, f32[64,128]{1,0:T(8,128)}, f32[64,128]{1,0:T(8,128)}, bf16[1,256,128]{2,1,0:T(8,128)(2,1)}) custom-call(f32[1,64,128]{2,1,0:T(8,128)} %get-tuple-element.10.refs_0_, f32[1,64,128]{2,1,0:T(8,128)} %get-tuple-element.11.refs_1_, f32[64,128]{1,0:T(8,128)} %get-tuple-element.12.refs_2_, ...), custom_call_target="tpu_custom_call" | custom-call | tf_op jit(solution)/shard_map/pallas_call | solution.py:458
